TPU v7x, 512 devices: a whole 4x4x16 slice. The times are simulated.
512 devices in a mesh: inst: 32 (over x_hi, z), tp: 16 (over x_lo, y, core).
Axes of the slice: x: 4 (x_hi: 2, x_lo: 2; x = x_hi * 2 + x_lo), y: 4, z: 16, core: 2. Of those that a mesh axis runs over, the one named last changes fastest.
Arguments:
- kv_pool: bfloat16 [1792, 16, 2, 128, 128], P('inst', 'tp'), may hold values from -4 to 4, as said below
- block_table: int32 [192, 8], P('inst'), may hold values from 0 to 55, as said below
- mig_table: int32 [32, 8], P('inst'), may hold values from 0 to 55, as said below
- query_stay: bfloat16 [192, 8192], P('inst', 'tp'), may hold values from -8 to 8
- query_mig: bfloat16 [32, 8192], P('inst', 'tp'), may hold values from -8 to 8
- new_stay: bfloat16 [192, 16, 2, 128], P('inst', 'tp'), may hold values from -4 to 4, as said below
- new_mig: bfloat16 [32, 16, 2, 128], P('inst', 'tp'), may hold values from -4 to 4, as said below
- len_stay: int32 [192], P('inst'), may hold values from 1 to 1024, as said below
- len_mig: int32 [32], P('inst'), may hold values from 1 to 1024, as said below
- hidden_stay: bfloat16 [192, 8192], P('inst', 'tp'), may hold values from -60 to 60
- hidden_mig: bfloat16 [32, 8192], P('inst', 'tp'), may hold values from -60 to 60
- norm_gain: bfloat16 [8192], P('tp'), may hold values from 0.099609375 to 1.8984375
- partner_mask: int32 [1], replicated, may hold values from 1 to 31
Outputs:
- attended: bfloat16 [224, 8192], P('inst', 'tp')
- arrived_pages: bfloat16 [32, 8, 16, 2, 128, 128], P('inst', None, 'tp')
- normed: bfloat16 [224, 8192], P('inst', 'tp')
Inputs may be any that keep to these rules, and one draw needn't show every extreme that they name: Each instance's block_table and mig_table rows together name each of its 56 local pages exactly once. `mig_table`: local page numbers, as in block_table. `len_stay`: lengths count cached tokens with the new one. `len_mig`: lengths count cached tokens with the new one. `kv_pool`: slot s holds kv head s // 2; slots of one head are equal. `new_stay`: slots of one kv head are equal. `new_mig`: slots of one kv head are equal. Instance i is matched with instance i XOR partner_mask[0].
All inputs are finite; a program needn't handle non-finite values.
Results may differ from a plain program's by a relative error of at most 0.0047.
Values may be sent and summed in bfloat16 or wider, within the bound.
A program may use at most 64 MiB of HBM per device.

v0:
```python
import jax
import jax.numpy as jnp
from jax import lax
from jax.sharding import PartitionSpec as P

D = 8192


def as_sent(shard):
    return jax.tree.map(lambda a: a.astype(jnp.bfloat16) if a.dtype == jnp.float32 else a, shard)


def swapped_2(shard, axis, bit):
    return lax.ppermute(shard, axis, [(i, i ^ 1 << bit) for i in range(lax.axis_size(axis))])


def write_token(pages, new_kv, length):
    page_count = pages.shape[0]
    page_size = pages.shape[3]
    shape = (page_count, 1, 1, page_size, 1)
    position = lax.broadcasted_iota(jnp.int32, shape, 0) * page_size + lax.broadcasted_iota(
        jnp.int32, shape, 3
    )
    return jnp.where(position == length - 1, new_kv[None, :, :, None, :], pages)


def attend_one(query, pages, length):
    page_count = pages.shape[0]
    slot_count = pages.shape[1]
    page_size = pages.shape[3]
    head_size = pages.shape[4]
    group_size = query.shape[0] // (slot_count * head_size)
    queries = query.reshape(slot_count, group_size, head_size)
    scores = jnp.einsum(
        "sgd,pstd->sgpt", queries, pages[:, :, 0], preferred_element_type=jnp.float32
    ) * head_size ** (-0.5)
    shape = (1, 1, page_count, page_size)
    position = lax.broadcasted_iota(jnp.int32, shape, 2) * page_size + lax.broadcasted_iota(
        jnp.int32, shape, 3
    )
    visible = position < length
    scores = jnp.where(visible, scores, -1e30)
    highest = jnp.max(scores, axis=(2, 3), keepdims=True)
    weights = jnp.where(visible, jnp.exp(scores - highest), 0.0)
    weights = (weights / jnp.sum(weights, axis=(2, 3), keepdims=True)).astype(jnp.bfloat16)
    mixed = jnp.einsum(
        "sgpt,pstd->sgd", weights, pages[:, :, 1], preferred_element_type=jnp.float32
    )
    return mixed.reshape(-1).astype(jnp.bfloat16)


def local(
    kv_pool,
    block_table,
    mig_table,
    query_stay,
    query_mig,
    new_stay,
    new_mig,
    len_stay,
    len_mig,
    hidden_stay,
    hidden_mig,
    norm_gain,
    partner_mask,
):
    pattern = partner_mask[0]
    bit_count = lax.axis_size("inst").bit_length() - 1
    bit_order = list(range(bit_count))

    def follow(payload, mover):
        for bit_index in bit_order:
            swapped = mover(payload, bit_index)
            chosen = jnp.bitwise_and(jnp.right_shift(pattern, bit_index), 1) == 1
            payload = tuple(
                (jnp.where(chosen, after, before) for before, after in zip(payload, swapped))
            )
        return payload

    leaving = jax.vmap(write_token)(kv_pool[mig_table], new_mig, len_mig)
    staying = jax.vmap(write_token)(kv_pool[block_table], new_stay, len_stay)
    arrived, query_in, length_in, hidden_in = follow(
        (leaving, query_mig, len_mig, hidden_mig),
        lambda payload, bit_index: swapped_2(
            (payload[0], payload[1], as_sent(payload[2]), payload[3]), "inst", bit_index
        ),
    )
    mixed_stay = jax.vmap(attend_one)(query_stay, staying, len_stay)
    mixed_in = jax.vmap(attend_one)(query_in, arrived, length_in)
    attended = jnp.concatenate([mixed_stay, mixed_in], axis=0)
    residual = jnp.concatenate([hidden_stay, hidden_in], axis=0).astype(jnp.float32)
    squares = lax.psum(jnp.sum(residual * residual, axis=1), "tp")
    row_scale = lax.rsqrt(squares / D + 1e-05)
    normed = (residual * row_scale[:, None] * norm_gain.astype(jnp.float32)).astype(jnp.bfloat16)
    return (attended, arrived, normed)


def solution(mesh):
    return jax.shard_map(
        local,
        mesh=mesh,
        in_specs=(
            P("inst", "tp", None, None, None),
            P("inst", None),
            P("inst", None),
            P("inst", "tp"),
            P("inst", "tp"),
            P("inst", "tp", None, None),
            P("inst", "tp", None, None),
            P("inst"),
            P("inst"),
            P("inst", "tp"),
            P("inst", "tp"),
            P("tp"),
            P(),
        ),
        out_specs=(P("inst", "tp"), P("inst", None, "tp", None, None, None), P("inst", "tp")),
        check_vma=False,
    )
```

profile of v0, /device:TPU:1, one launch (start us, length us, event | category | flops | bytes accessed | tf_op | source)
XLA Modules:
  0.0 231.0 jit_solution(13827892969822890440)
XLA Ops:
  0.6 4.4 %collective-permute-start = (s32[1]{0:T(128)}, s32[1]{0:T(128)}, u32[]{:S(2)}, u32[]{:S(2)}) collective-permute-start(s32[1]{0:T(128)} %param.21), channel_id=1, source_target_pairs={{0,16},{16,0},{32,48},{48,32},{64,80},{80,64},{96,112},{112,96},{1... | collective-permute-start | bytes 20 | tf_op jit(solution)/shard_map/ppermute | solution.py:14
  6.9 3.4 %collective-permute-start.15 = (bf16[1,512]{1,0:T(2,128)(2,1)}, bf16[1,512]{1,0:T(2,128)(2,1)S(1)}, u32[]{:S(2)}, u32[]{:S(2)}) collective-permute-start(bf16[1,512]{1,0:T(2,128)(2,1)} %param.23), channel_id=1, source_target_pairs={{0,16},{16,0},{32,48},{48,32},{64,80},{80,64},{96,112},{112,96},{1... | collective-permute-start | bytes 3080 | tf_op jit(solution)/shard_map/ppermute | solution.py:14
  13.8 3.4 %gather_fusion.1 = bf16[8,2,128,128]{3,2,1,0:T(8,128)(2,1)} fusion(bf16[56,2,128,128]{3,2,1,0:T(8,128)(2,1)} %bitcast.82, s32[1024]{0:T(1024)S(1)} %pad_clamp_fusion), kind=kCustom, calls=%fused_computation.1 | custom fusion | bytes 1048608 | tf_op jit(solution)/shard_map/gather | solution.py:80
  17.2 4.7 %gather_fusion = bf16[48,2,128,128]{3,2,1,0:T(8,128)(2,1)} fusion(bf16[56,2,128,128]{3,2,1,0:T(8,128)(2,1)} %bitcast.83, s32[1024]{0:T(1024)S(1)} %pad_clamp_fusion.1), kind=kCustom, calls=%fused_computation | custom fusion | bytes 6291648 | tf_op jit(solution)/shard_map/gather | solution.py:81
  26.0 5.6 %collective-permute-start.1 = (s32[1]{0:T(128)}, s32[1]{0:T(128)}, u32[]{:S(2)}, u32[]{:S(2)}) collective-permute-start(s32[1]{0:T(128)} %select_n.162), channel_id=1, source_target_pairs={{0,32},{16,48},{32,0},{48,16},{64,96},{80,112},{96,64},{112,80},{1... | collective-permute-start | bytes 20 | tf_op jit(solution)/shard_map/ppermute | solution.py:14
  32.6 9.5 %collective-permute-start.2 = (s32[1]{0:T(128)}, s32[1]{0:T(128)}, u32[]{:S(2)}, u32[]{:S(2)}) collective-permute-start(s32[1]{0:T(128)} %select_n.163), channel_id=1, source_target_pairs={{0,64},{16,80},{32,96},{48,112},{64,0},{80,16},{96,32},{112,48},{1... | collective-permute-start | bytes 20 | tf_op jit(solution)/shard_map/ppermute | solution.py:14
  43.1 13.1 %collective-permute-start.3 = (s32[1]{0:T(128)}, s32[1]{0:T(128)}, u32[]{:S(2)}, u32[]{:S(2)}) collective-permute-start(s32[1]{0:T(128)} %select_n.164), channel_id=1, source_target_pairs={{0,128},{16,144},{32,160},{48,176},{64,192},{80,208},{96,224},{112... | collective-permute-start | bytes 20 | tf_op jit(solution)/shard_map/ppermute | solution.py:14
  57.1 5.4 %collective-permute-start.4 = (s32[1]{0:T(128)}, s32[1]{0:T(128)}, u32[]{:S(2)}, u32[]{:S(2)}) collective-permute-start(s32[1]{0:T(128)} %select_n.165), channel_id=1, source_target_pairs={{0,256},{16,272},{32,288},{48,304},{64,320},{80,336},{96,352},{112... | collective-permute-start | bytes 20 | tf_op jit(solution)/shard_map/ppermute | solution.py:14
  63.9 2.6 %collective-permute-start.10 = (bf16[1,8,1,2,128,128]{5,4,1,3,2,0:T(8,128)(2,1)S(1)}, bf16[1,8,1,2,128,128]{5,4,1,3,2,0:T(8,128)(2,1)S(1)}, u32[]{:S(2)}, u32[]{:S(2)}) collective-permute-start(bf16[1,8,1,2,128,128]{5,4,1,3,2,0:T(8,128)(2,1)S(1)} %bitcast_select_fusion), channel_id=1, source_target_pairs={{0,16},{16,0},{32,48},{48,32},{64,80},{80,64},{96,112},{112,96},{1... | collective-permute-start | bytes 1572872 | tf_op jit(solution)/shard_map/ppermute | solution.py:14
  67.8 6.0 %collective-permute-done.10 = bf16[1,8,1,2,128,128]{5,4,1,3,2,0:T(8,128)(2,1)S(1)} collective-permute-done((bf16[1,8,1,2,128,128]{5,4,1,3,2,0:T(8,128)(2,1)S(1)}, bf16[1,8,1,2,128,128]{5,4,1,3,2,0:T(8,128)(2,1)S(1)}, u32[]{:S(2)}, u32[]{:S(2)}) %collective-permute-start.10) | collective-permute-done | bytes 524320 | tf_op jit(solution)/shard_map/ppermute | solution.py:14
  74.1 4.0 %collective-permute-start.11 = (bf16[1,8,1,2,128,128]{5,4,1,3,2,0:T(8,128)(2,1)S(1)}, bf16[1,8,1,2,128,128]{5,4,1,3,2,0:T(8,128)(2,1)S(1)}, u32[]{:S(2)}, u32[]{:S(2)}) collective-permute-start(bf16[1,8,1,2,128,128]{5,4,1,3,2,0:T(8,128)(2,1)S(1)} %broadcast_select_fusion.1), channel_id=1, source_target_pairs={{0,32},{16,48},{32,0},{48,16},{64,96},{80,112},{96,64},{112,80},{1... | collective-permute-start | bytes 1572872 | tf_op jit(solution)/shard_map/ppermute | solution.py:14
  80.3 4.0 %collective-permute-start.16 = (bf16[1,512]{1,0:T(2,128)(2,1)S(1)}, bf16[1,512]{1,0:T(2,128)(2,1)S(1)}, u32[]{:S(2)}, u32[]{:S(2)}) collective-permute-start(bf16[1,512]{1,0:T(2,128)(2,1)S(1)} %broadcast_select_fusion.6), channel_id=1, source_target_pairs={{0,32},{16,48},{32,0},{48,16},{64,96},{80,112},{96,64},{112,80},{1... | collective-permute-start | bytes 3080 | tf_op jit(solution)/shard_map/ppermute | solution.py:14
  84.3 13.3 %collective-permute-done.6 = bf16[1,512]{1,0:T(2,128)(2,1)S(1)} collective-permute-done((bf16[1,512]{1,0:T(2,128)(2,1)S(1)}, bf16[1,512]{1,0:T(2,128)(2,1)S(1)}, u32[]{:S(2)}, u32[]{:S(2)}) %collective-permute-start.6) | collective-permute-done | bytes 1056 | tf_op jit(solution)/shard_map/ppermute | solution.py:14
  97.6 8.8 %collective-permute-start.7 = (bf16[1,512]{1,0:T(2,128)(2,1)S(1)}, bf16[1,512]{1,0:T(2,128)(2,1)S(1)}, u32[]{:S(2)}, u32[]{:S(2)}) collective-permute-start(bf16[1,512]{1,0:T(2,128)(2,1)S(1)} %broadcast_select_fusion.9), channel_id=1, source_target_pairs={{0,64},{16,80},{32,96},{48,112},{64,0},{80,16},{96,32},{112,48},{1... | collective-permute-start | bytes 3080 | tf_op jit(solution)/shard_map/ppermute | solution.py:14
  108.4 7.3 %collective-permute-start.17 = (bf16[1,512]{1,0:T(2,128)(2,1)S(1)}, bf16[1,512]{1,0:T(2,128)(2,1)S(1)}, u32[]{:S(2)}, u32[]{:S(2)}) collective-permute-start(bf16[1,512]{1,0:T(2,128)(2,1)S(1)} %broadcast_select_fusion.8), channel_id=1, source_target_pairs={{0,64},{16,80},{32,96},{48,112},{64,0},{80,16},{96,32},{112,48},{1... | collective-permute-start | bytes 3080 | tf_op jit(solution)/shard_map/ppermute | solution.py:14
  115.8 9.3 %collective-permute-start.8 = (bf16[1,512]{1,0:T(2,128)(2,1)S(1)}, bf16[1,512]{1,0:T(2,128)(2,1)S(1)}, u32[]{:S(2)}, u32[]{:S(2)}) collective-permute-start(bf16[1,512]{1,0:T(2,128)(2,1)S(1)} %broadcast_select_fusion.11), channel_id=1, source_target_pairs={{0,128},{16,144},{32,160},{48,176},{64,192},{80,208},{96,224},{112... | collective-permute-start | bytes 3080 | tf_op jit(solution)/shard_map/ppermute | solution.py:14
  125.1 33.8 %collective-permute-done.17 = bf16[1,512]{1,0:T(2,128)(2,1)S(1)} collective-permute-done((bf16[1,512]{1,0:T(2,128)(2,1)S(1)}, bf16[1,512]{1,0:T(2,128)(2,1)S(1)}, u32[]{:S(2)}, u32[]{:S(2)}) %collective-permute-start.17) | collective-permute-done | bytes 1056 | tf_op jit(solution)/shard_map/ppermute | solution.py:14
  158.9 9.3 %collective-permute-start.18 = (bf16[1,512]{1,0:T(2,128)(2,1)S(1)}, bf16[1,512]{1,0:T(2,128)(2,1)S(1)}, u32[]{:S(2)}, u32[]{:S(2)}) collective-permute-start(bf16[1,512]{1,0:T(2,128)(2,1)S(1)} %broadcast_select_fusion.10), channel_id=1, source_target_pairs={{0,128},{16,144},{32,160},{48,176},{64,192},{80,208},{96,224},{112... | collective-permute-start | bytes 3080 | tf_op jit(solution)/shard_map/ppermute | solution.py:14
  168.2 4.7 %collective-permute-start.13 = (bf16[1,8,1,2,128,128]{5,4,1,3,2,0:T(8,128)(2,1)S(1)}, bf16[1,8,1,2,128,128]{5,4,1,3,2,0:T(8,128)(2,1)S(1)}, u32[]{:S(2)}, u32[]{:S(2)}) collective-permute-start(bf16[1,8,1,2,128,128]{5,4,1,3,2,0:T(8,128)(2,1)S(1)} %broadcast_select_fusion.3), channel_id=1, source_target_pairs={{0,128},{16,144},{32,160},{48,176},{64,192},{80,208},{96,224},{112... | collective-permute-start | bytes 1572872 | tf_op jit(solution)/shard_map/ppermute | solution.py:14
  173.0 4.7 %collective-permute-start.19 = (bf16[1,512]{1,0:T(2,128)(2,1)S(1)}, bf16[1,512]{1,0:T(2,128)(2,1)S(1)}, u32[]{:S(2)}, u32[]{:S(2)}) collective-permute-start(bf16[1,512]{1,0:T(2,128)(2,1)S(1)} %broadcast_select_fusion.12), channel_id=1, source_target_pairs={{0,256},{16,272},{32,288},{48,304},{64,320},{80,336},{96,352},{112... | collective-permute-start | bytes 3080 | tf_op jit(solution)/shard_map/ppermute | solution.py:14
  179.0 4.6 %collective-permute-start.9 = (bf16[1,512]{1,0:T(2,128)(2,1)S(1)}, bf16[1,512]{1,0:T(2,128)(2,1)S(1)}, u32[]{:S(2)}, u32[]{:S(2)}) collective-permute-start(bf16[1,512]{1,0:T(2,128)(2,1)S(1)} %broadcast_select_fusion.13), channel_id=1, source_target_pairs={{0,256},{16,272},{32,288},{48,304},{64,320},{80,336},{96,352},{112... | collective-permute-start | bytes 3080 | tf_op jit(solution)/shard_map/ppermute | solution.py:14
  183.6 29.6 %psum.7 = f32[7]{0:T(128)S(1)} all-reduce(f32[7]{0:T(128)S(1)} %fusion.16), channel_id=1, replica_groups=mesh['inst'=32,'tp'=16] {'tp'}, use_global_device_ids=true, to_apply=%region_5.6 | all-reduce | flops 7 | bytes 56 | tf_op jit(solution)/shard_map/psum | solution.py:92
  213.3 2.7 %collective-permute-start.14 = (bf16[1,8,1,2,128,128]{5,4,1,3,2,0:T(8,128)(2,1)S(1)}, bf16[1,8,1,2,128,128]{5,4,1,3,2,0:T(8,128)(2,1)S(1)}, u32[]{:S(2)}, u32[]{:S(2)}) collective-permute-start(bf16[1,8,1,2,128,128]{5,4,1,3,2,0:T(8,128)(2,1)S(1)} %broadcast_select_fusion.4), channel_id=1, source_target_pairs={{0,256},{16,272},{32,288},{48,304},{64,320},{80,336},{96,352},{112... | collective-permute-start | bytes 1572872 | tf_op jit(solution)/shard_map/ppermute | solution.py:14
  216.6 12.1 %collective-permute-done.14 = bf16[1,8,1,2,128,128]{5,4,1,3,2,0:T(8,128)(2,1)S(1)} collective-permute-done((bf16[1,8,1,2,128,128]{5,4,1,3,2,0:T(8,128)(2,1)S(1)}, bf16[1,8,1,2,128,128]{5,4,1,3,2,0:T(8,128)(2,1)S(1)}, u32[]{:S(2)}, u32[]{:S(2)}) %collective-permute-start.14) | collective-permute-done | bytes 524320 | tf_op jit(solution)/shard_map/ppermute | solution.py:14
  (81 shorter events, 19.4 us)
Async XLA Ops:
  0.6 24.8 %collective-permute-start = (s32[1]{0:T(128)}, s32[1]{0:T(128)}, u32[]{:S(2)}, u32[]{:S(2)}) collective-permute-start(s32[1]{0:T(128)} %param.21), channel_id=1, source_target_pairs={{0,16},{16,0},{32,48},{48,32},{64,80},{80,64},{96,112},{112,96},{1... | collective-permute-start | bytes 20 | tf_op jit(solution)/shard_map/ppermute | solution.py:14
  5.0 73.0 %collective-permute-start.5 = (bf16[1,512]{1,0:T(2,128)(2,1)}, bf16[1,512]{1,0:T(2,128)(2,1)S(1)}, u32[]{:S(2)}, u32[]{:S(2)}) collective-permute-start(bf16[1,512]{1,0:T(2,128)(2,1)} %param.17), channel_id=1, source_target_pairs={{0,16},{16,0},{32,48},{48,32},{64,80},{80,64},{96,112},{112,96},{1... | collective-permute-start | bytes 3080 | tf_op jit(solution)/shard_map/ppermute | solution.py:14
  6.9 73.4 %collective-permute-start.15 = (bf16[1,512]{1,0:T(2,128)(2,1)}, bf16[1,512]{1,0:T(2,128)(2,1)S(1)}, u32[]{:S(2)}, u32[]{:S(2)}) collective-permute-start(bf16[1,512]{1,0:T(2,128)(2,1)} %param.23), channel_id=1, source_target_pairs={{0,16},{16,0},{32,48},{48,32},{64,80},{80,64},{96,112},{112,96},{1... | collective-permute-start | bytes 3080 | tf_op jit(solution)/shard_map/ppermute | solution.py:14
  24.3 39.5 %copy-start = (bf16[8,2,128,128]{3,2,1,0:T(8,128)(2,1)S(1)}, bf16[8,2,128,128]{3,2,1,0:T(8,128)(2,1)}, u32[]{:S(2)}) copy-start(bf16[8,2,128,128]{3,2,1,0:T(8,128)(2,1)} %gather_fusion.1) | copy-start | bytes 1572868
  24.3 39.4 %copy-start.4 = (bf16[1,1,2,128]{3,2,1,0:T(2,128)(2,1)S(1)}, bf16[1,1,2,128]{3,2,1,0:T(2,128)(2,1)}, u32[]{:S(2)}) copy-start(bf16[1,1,2,128]{3,2,1,0:T(2,128)(2,1)} %param.19) | copy-start | bytes 1540
  25.5 42.4 %copy-start.7 = (bf16[512]{0:T(512)(128)(2,1)S(1)}, bf16[512]{0:T(512)(128)(2,1)}, u32[]{:S(2)}) copy-start(bf16[512]{0:T(512)(128)(2,1)} %param.24) | copy-start | bytes 3076
  26.0 5.9 %collective-permute-start.1 = (s32[1]{0:T(128)}, s32[1]{0:T(128)}, u32[]{:S(2)}, u32[]{:S(2)}) collective-permute-start(s32[1]{0:T(128)} %select_n.162), channel_id=1, source_target_pairs={{0,32},{16,48},{32,0},{48,16},{64,96},{80,112},{96,64},{112,80},{1... | collective-permute-start | bytes 20 | tf_op jit(solution)/shard_map/ppermute | solution.py:14
  32.6 9.8 %collective-permute-start.2 = (s32[1]{0:T(128)}, s32[1]{0:T(128)}, u32[]{:S(2)}, u32[]{:S(2)}) collective-permute-start(s32[1]{0:T(128)} %select_n.163), channel_id=1, source_target_pairs={{0,64},{16,80},{32,96},{48,112},{64,0},{80,16},{96,32},{112,48},{1... | collective-permute-start | bytes 20 | tf_op jit(solution)/shard_map/ppermute | solution.py:14
  43.1 13.4 %collective-permute-start.3 = (s32[1]{0:T(128)}, s32[1]{0:T(128)}, u32[]{:S(2)}, u32[]{:S(2)}) collective-permute-start(s32[1]{0:T(128)} %select_n.164), channel_id=1, source_target_pairs={{0,128},{16,144},{32,160},{48,176},{64,192},{80,208},{96,224},{112... | collective-permute-start | bytes 20 | tf_op jit(solution)/shard_map/ppermute | solution.py:14
  57.1 5.9 %collective-permute-start.4 = (s32[1]{0:T(128)}, s32[1]{0:T(128)}, u32[]{:S(2)}, u32[]{:S(2)}) collective-permute-start(s32[1]{0:T(128)} %select_n.165), channel_id=1, source_target_pairs={{0,256},{16,272},{32,288},{48,304},{64,320},{80,336},{96,352},{112... | collective-permute-start | bytes 20 | tf_op jit(solution)/shard_map/ppermute | solution.py:14
  63.9 9.9 %collective-permute-start.10 = (bf16[1,8,1,2,128,128]{5,4,1,3,2,0:T(8,128)(2,1)S(1)}, bf16[1,8,1,2,128,128]{5,4,1,3,2,0:T(8,128)(2,1)S(1)}, u32[]{:S(2)}, u32[]{:S(2)}) collective-permute-start(bf16[1,8,1,2,128,128]{5,4,1,3,2,0:T(8,128)(2,1)S(1)} %bitcast_select_fusion), channel_id=1, source_target_pairs={{0,16},{16,0},{32,48},{48,32},{64,80},{80,64},{96,112},{112,96},{1... | collective-permute-start | bytes 1572872 | tf_op jit(solution)/shard_map/ppermute | solution.py:14
  67.4 111.4 %copy-start.1 = (bf16[6,512]{1,0:T(8,128)(2,1)S(1)}, bf16[6,512]{1,0:T(8,128)(2,1)}, u32[]{:S(2)}) copy-start(bf16[6,512]{1,0:T(8,128)(2,1)} %param.22) | copy-start | bytes 18436
  74.1 32.3 %collective-permute-start.11 = (bf16[1,8,1,2,128,128]{5,4,1,3,2,0:T(8,128)(2,1)S(1)}, bf16[1,8,1,2,128,128]{5,4,1,3,2,0:T(8,128)(2,1)S(1)}, u32[]{:S(2)}, u32[]{:S(2)}) collective-permute-start(bf16[1,8,1,2,128,128]{5,4,1,3,2,0:T(8,128)(2,1)S(1)} %broadcast_select_fusion.1), channel_id=1, source_target_pairs={{0,32},{16,48},{32,0},{48,16},{64,96},{80,112},{96,64},{112,80},{1... | collective-permute-start | bytes 1572872 | tf_op jit(solution)/shard_map/ppermute | solution.py:14
  78.1 19.5 %collective-permute-start.6 = (bf16[1,512]{1,0:T(2,128)(2,1)S(1)}, bf16[1,512]{1,0:T(2,128)(2,1)S(1)}, u32[]{:S(2)}, u32[]{:S(2)}) collective-permute-start(bf16[1,512]{1,0:T(2,128)(2,1)S(1)} %broadcast_select_fusion.7), channel_id=1, source_target_pairs={{0,32},{16,48},{32,0},{48,16},{64,96},{80,112},{96,64},{112,80},{1... | collective-permute-start | bytes 3080 | tf_op jit(solution)/shard_map/ppermute | solution.py:14
  80.3 28.1 %collective-permute-start.16 = (bf16[1,512]{1,0:T(2,128)(2,1)S(1)}, bf16[1,512]{1,0:T(2,128)(2,1)S(1)}, u32[]{:S(2)}, u32[]{:S(2)}) collective-permute-start(bf16[1,512]{1,0:T(2,128)(2,1)S(1)} %broadcast_select_fusion.6), channel_id=1, source_target_pairs={{0,32},{16,48},{32,0},{48,16},{64,96},{80,112},{96,64},{112,80},{1... | collective-permute-start | bytes 3080 | tf_op jit(solution)/shard_map/ppermute | solution.py:14
  97.6 18.1 %collective-permute-start.7 = (bf16[1,512]{1,0:T(2,128)(2,1)S(1)}, bf16[1,512]{1,0:T(2,128)(2,1)S(1)}, u32[]{:S(2)}, u32[]{:S(2)}) collective-permute-start(bf16[1,512]{1,0:T(2,128)(2,1)S(1)} %broadcast_select_fusion.9), channel_id=1, source_target_pairs={{0,64},{16,80},{32,96},{48,112},{64,0},{80,16},{96,32},{112,48},{1... | collective-permute-start | bytes 3080 | tf_op jit(solution)/shard_map/ppermute | solution.py:14
  106.5 61.7 %collective-permute-start.12 = (bf16[1,8,1,2,128,128]{5,4,1,3,2,0:T(8,128)(2,1)S(1)}, bf16[1,8,1,2,128,128]{5,4,1,3,2,0:T(8,128)(2,1)S(1)}, u32[]{:S(2)}, u32[]{:S(2)}) collective-permute-start(bf16[1,8,1,2,128,128]{5,4,1,3,2,0:T(8,128)(2,1)S(1)} %broadcast_select_fusion.2), channel_id=1, source_target_pairs={{0,64},{16,80},{32,96},{48,112},{64,0},{80,16},{96,32},{112,48},{1... | collective-permute-start | bytes 1572872 | tf_op jit(solution)/shard_map/ppermute | solution.py:14
  108.4 50.4 %collective-permute-start.17 = (bf16[1,512]{1,0:T(2,128)(2,1)S(1)}, bf16[1,512]{1,0:T(2,128)(2,1)S(1)}, u32[]{:S(2)}, u32[]{:S(2)}) collective-permute-start(bf16[1,512]{1,0:T(2,128)(2,1)S(1)} %broadcast_select_fusion.8), channel_id=1, source_target_pairs={{0,64},{16,80},{32,96},{48,112},{64,0},{80,16},{96,32},{112,48},{1... | collective-permute-start | bytes 3080 | tf_op jit(solution)/shard_map/ppermute | solution.py:14
  115.8 61.9 %collective-permute-start.8 = (bf16[1,512]{1,0:T(2,128)(2,1)S(1)}, bf16[1,512]{1,0:T(2,128)(2,1)S(1)}, u32[]{:S(2)}, u32[]{:S(2)}) collective-permute-start(bf16[1,512]{1,0:T(2,128)(2,1)S(1)} %broadcast_select_fusion.11), channel_id=1, source_target_pairs={{0,128},{16,144},{32,160},{48,176},{64,192},{80,208},{96,224},{112... | collective-permute-start | bytes 3080 | tf_op jit(solution)/shard_map/ppermute | solution.py:14
  158.9 14.1 %collective-permute-start.18 = (bf16[1,512]{1,0:T(2,128)(2,1)S(1)}, bf16[1,512]{1,0:T(2,128)(2,1)S(1)}, u32[]{:S(2)}, u32[]{:S(2)}) collective-permute-start(bf16[1,512]{1,0:T(2,128)(2,1)S(1)} %broadcast_select_fusion.10), channel_id=1, source_target_pairs={{0,128},{16,144},{32,160},{48,176},{64,192},{80,208},{96,224},{112... | collective-permute-start | bytes 3080 | tf_op jit(solution)/shard_map/ppermute | solution.py:14
  168.2 45.0 %collective-permute-start.13 = (bf16[1,8,1,2,128,128]{5,4,1,3,2,0:T(8,128)(2,1)S(1)}, bf16[1,8,1,2,128,128]{5,4,1,3,2,0:T(8,128)(2,1)S(1)}, u32[]{:S(2)}, u32[]{:S(2)}) collective-permute-start(bf16[1,8,1,2,128,128]{5,4,1,3,2,0:T(8,128)(2,1)S(1)} %broadcast_select_fusion.3), channel_id=1, source_target_pairs={{0,128},{16,144},{32,160},{48,176},{64,192},{80,208},{96,224},{112... | collective-permute-start | bytes 1572872 | tf_op jit(solution)/shard_map/ppermute | solution.py:14
  173.0 5.8 %collective-permute-start.19 = (bf16[1,512]{1,0:T(2,128)(2,1)S(1)}, bf16[1,512]{1,0:T(2,128)(2,1)S(1)}, u32[]{:S(2)}, u32[]{:S(2)}) collective-permute-start(bf16[1,512]{1,0:T(2,128)(2,1)S(1)} %broadcast_select_fusion.12), channel_id=1, source_target_pairs={{0,256},{16,272},{32,288},{48,304},{64,320},{80,336},{96,352},{112... | collective-permute-start | bytes 3080 | tf_op jit(solution)/shard_map/ppermute | solution.py:14
  179.0 37.0 %collective-permute-start.9 = (bf16[1,512]{1,0:T(2,128)(2,1)S(1)}, bf16[1,512]{1,0:T(2,128)(2,1)S(1)}, u32[]{:S(2)}, u32[]{:S(2)}) collective-permute-start(bf16[1,512]{1,0:T(2,128)(2,1)S(1)} %broadcast_select_fusion.13), channel_id=1, source_target_pairs={{0,256},{16,272},{32,288},{48,304},{64,320},{80,336},{96,352},{112... | collective-permute-start | bytes 3080 | tf_op jit(solution)/shard_map/ppermute | solution.py:14
  213.3 15.5 %collective-permute-start.14 = (bf16[1,8,1,2,128,128]{5,4,1,3,2,0:T(8,128)(2,1)S(1)}, bf16[1,8,1,2,128,128]{5,4,1,3,2,0:T(8,128)(2,1)S(1)}, u32[]{:S(2)}, u32[]{:S(2)}) collective-permute-start(bf16[1,8,1,2,128,128]{5,4,1,3,2,0:T(8,128)(2,1)S(1)} %broadcast_select_fusion.4), channel_id=1, source_target_pairs={{0,256},{16,272},{32,288},{48,304},{64,320},{80,336},{96,352},{112... | collective-permute-start | bytes 1572872 | tf_op jit(solution)/shard_map/ppermute | solution.py:14
  (5 other events, 31.8 us)
where the time goes:
time: 232 us; the launch traced here: 231 us
  starting transfers between devices  109 us (47%)
  waiting for transfers between devices  67.9 us (29%)
  blocking collectives  29.6 us (13%)
  local copies, waits for them, and re-layouts  11.3 us (5%)
  other arithmetic  6 us (3%)
  between operations  5.51 us (2%)
    ppermute x20, starting transfers between devices, swapped_2(): lax.ppermute(shard, axis, [(i, i ^ 1 << bit) for i in range(lax.axis_size...  109 us
    ppermute x20, waiting for transfers between devices, swapped_2(): lax.ppermute(shard, axis, [(i, i ^ 1 << bit) for i in range(lax.axis_size...  67.9 us
    psum x1, blocking collectives, local(): squares = lax.psum(jnp.sum(residual * residual, axis=1), 'tp')  29.6 us
    gather x2, local copies, waits for them, and re-layouts, local(): staying = jax.vmap(write_token)(kv_pool[block_table], new_stay, len_stay)  6.86 us
  transfers between devices with their start and end apart: 20, of which 9 were waited for; matrix products, arithmetic and copies ran while one was open for 7% of the time, Pallas kernels for 0%

commit v1 on v0

v1 whole, which is shorter than its diff:
```python
import functools

import jax
import jax.numpy as jnp
from jax import lax
from jax.experimental import pallas as pl
from jax.experimental.pallas import tpu as pltpu
from jax.sharding import PartitionSpec as P

MESH = pl.DeviceIdType.MESH
D = 8192
LANES = 128
GROUP = 4
PARTS = 8


def flipped(index, mask):
    bit = 1
    total = index
    while bit <= mask:
        if mask & bit:
            total = total + bit - 2 * bit * ((index // bit) % 2)
        bit *= 2
    return total


def attend(pool, table, row, query, new_kv, length):
    pages = table.shape[1]
    page = pool.shape[2]
    new_key = new_kv[0:1].astype(jnp.float32)
    new_value = new_kv[1:2].astype(jnp.float32)
    scale = LANES ** (-0.5)
    new_score = jnp.sum(query.astype(jnp.float32) * new_key, axis=1, keepdims=True) * scale
    column = lax.broadcasted_iota(jnp.int32, (query.shape[0], page), 1)
    scores = []
    for j in range(pages):
        score = lax.dot_general(
            query,
            pool[table[row, j], 0],
            (((1,), (1,)), ((), ())),
            preferred_element_type=jnp.float32,
        )
        score = score * scale
        position = column + j * page
        score = jnp.where(position == length - 1, new_score, score)
        scores.append(jnp.where(position < length, score, -1e30))
    highest = functools.reduce(jnp.maximum, scores)
    highest = jnp.max(highest, axis=1, keepdims=True)
    weights = [
        jnp.where(column + j * page < length, jnp.exp(s - highest), 0.0)
        for j, s in enumerate(scores)
    ]
    total = jnp.sum(functools.reduce(jnp.add, weights), axis=1, keepdims=True)
    mixed = jnp.zeros((query.shape[0], LANES), jnp.float32)
    last = jnp.zeros((query.shape[0], page), jnp.float32)
    for j, w in enumerate(weights):
        w = (w / total).astype(jnp.bfloat16).astype(jnp.float32)
        is_last = column + j * page == length - 1
        last = last + jnp.where(is_last, w, 0.0)
        w = jnp.where(is_last, 0.0, w).astype(jnp.bfloat16)
        mixed = mixed + jnp.dot(w, pool[table[row, j], 1], preferred_element_type=jnp.float32)
    return mixed + jnp.sum(last, axis=1, keepdims=True) * new_value


def kernel(
    mask,
    tp_bits,
    kv_ref,
    block_table,
    mig_table,
    len_stay,
    len_mig,
    query_stay,
    query_mig,
    new_stay,
    new_mig,
    hidden_stay,
    hidden_mig,
    gain,
    attended,
    arrived,
    normed,
    pool,
    out_pages,
    queries,
    mixed,
    rows,
    sums_out,
    sums_in,
    note_out,
    note_in,
    pool_sem,
    page_send,
    page_recv,
    pass_send,
    pass_recv,
    sum_send,
    sum_recv,
    note_send,
    note_recv,
):
    inst, tp = lax.axis_index("inst"), lax.axis_index("tp")
    core = tp % 2
    other = flipped(tp, 1)
    partner = flipped(inst, mask)
    stay = query_stay.shape[0]
    page_count, _, page, _ = pool.shape
    half = out_pages.shape[0]

    part = page_count // PARTS
    loads = [
        pltpu.make_async_copy(
            kv_ref.at[pl.ds(c * part, part), 0], pool.at[pl.ds(c * part, part)], pool_sem.at[c]
        )
        for c in range(PARTS)
    ]
    for load in loads:
        load.start()

    barrier = pltpu.get_barrier_semaphore()
    pl.semaphore_signal(barrier, inc=1, device_id=(partner, tp), device_id_type=MESH)
    for b in range(tp_bits):
        pl.semaphore_signal(
            barrier, inc=1, device_id=(inst, flipped(tp, 1 << b)), device_id_type=MESH
        )

    queries[...] = jnp.zeros_like(queries)
    rows[...] = jnp.zeros_like(rows)
    stay_q, mig_q = query_stay[...].astype(jnp.float32), query_mig[...].astype(jnp.float32)
    for r in range(stay + 1):
        line = mig_q if r == stay else stay_q[r : r + 1]
        for h in range(GROUP):
            queries[r, h : h + 1, :] = line[:, h * LANES : (h + 1) * LANES]
    rows[0:stay, :] = hidden_stay[...].astype(jnp.float32)
    rows[stay : stay + 1, :] = hidden_mig[...].astype(jnp.float32)
    square = rows[...] * rows[...]
    width = square.shape[1]
    sums_out[0] = sum(square[:, c : c + LANES] for c in range(0, width, LANES))

    for load in loads:
        load.wait()
    pl.semaphore_wait(barrier, tp_bits + 1)

    length = len_mig[0]
    new_line = new_mig[0, 0]
    position = lax.broadcasted_iota(jnp.int32, (page, LANES), 0)
    sends = []
    for j in range(half):
        at = mig_table[0, core * half + j]
        here = position == length - 1 - (core * half + j) * page
        for k in range(2):
            out_pages[j, k] = jnp.where(here, new_line[k : k + 1], pool[at, k])
        send = pltpu.make_async_remote_copy(
            src_ref=out_pages.at[j],
            dst_ref=arrived.at[0, core * half + j, 0],
            send_sem=page_send.at[j],
            recv_sem=page_recv.at[j],
            device_id=(partner, tp),
            device_id_type=MESH,
        )
        send.start()
        sends.append(send)

    def sum_step(b):
        bit = 1 << b
        return pltpu.make_async_remote_copy(
            src_ref=sums_out.at[b],
            dst_ref=sums_in.at[b],
            send_sem=sum_send.at[b],
            recv_sem=sum_recv.at[b],
            device_id=(inst, flipped(tp, bit)),
            device_id_type=MESH,
        )

    def attend_staying(r, _):
        mixed[r] = attend(
            pool, block_table, r, queries[r].astype(jnp.bfloat16), new_stay[r, 0], len_stay[r]
        )
        return 0

    step = sum_step(0)
    step.start()
    leaving = attend(
        pool, mig_table, 0, queries[stay].astype(jnp.bfloat16), new_line, length
    )
    step.wait()
    done = 0
    for b in range(1, tp_bits):
        sums_out[b] = sums_out[b - 1] + sums_in[b - 1]
        step = sum_step(b)
        step.start()
        upto = stay * b // (tp_bits - 1)
        lax.fori_loop(done, upto, attend_staying, 0)
        done = upto
        step.wait()
    sums = sums_out[tp_bits - 1] + sums_in[tp_bits - 1]
    mean_square = jnp.sum(sums, axis=1, keepdims=True) / D
    rows[...] = rows[...] * lax.rsqrt(mean_square + 1e-05) * gain[...].astype(jnp.float32)

    note_out[0:8, :] = leaving.astype(jnp.bfloat16)
    own = rows[stay : stay + 1, :]
    lines = [own[:, h * LANES : (h + 1) * LANES] for h in range(GROUP)]
    note_out[8:16, :] = jnp.concatenate(lines + lines, axis=0).astype(jnp.bfloat16)
    note = pltpu.make_async_remote_copy(
        src_ref=note_out,
        dst_ref=note_in,
        send_sem=note_send,
        recv_sem=note_recv,
        device_id=(partner, tp),
        device_id_type=MESH,
    )
    note.start()

    passes = []
    for j in range(half):
        sends[j].wait_recv()
        onward = pltpu.make_async_remote_copy(
            src_ref=arrived.at[0, core * half + j, 0],
            dst_ref=arrived.at[0, core * half + j, 0],
            send_sem=pass_send.at[j],
            recv_sem=pass_recv.at[j],
            device_id=(inst, other),
            device_id_type=MESH,
        )
        onward.start()
        passes.append(onward)

    note.wait()
    got = note_in[...].astype(jnp.float32)
    mixed[stay] = got[0:8]
    for h in range(GROUP):
        attended[:, h * LANES : (h + 1) * LANES] = mixed[:, h, :].astype(jnp.bfloat16)
        rows[stay : stay + 1, h * LANES : (h + 1) * LANES] = got[8 + h : 9 + h]
    normed[...] = rows[0 : stay + 1, :].astype(jnp.bfloat16)
    for send in sends:
        send.wait_send()
    for onward in passes:
        onward.wait()


def local(
    kv_pool,
    block_table,
    mig_table,
    query_stay,
    query_mig,
    new_stay,
    new_mig,
    len_stay,
    len_mig,
    hidden_stay,
    hidden_mig,
    norm_gain,
    partner_mask,
):
    page_count, _, _, page, head = kv_pool.shape
    stay, width = query_stay.shape
    slots = mig_table.shape[1]
    half = slots // 2
    tp_bits = lax.axis_size("tp").bit_length() - 1
    bf16, f32 = jnp.bfloat16, jnp.float32
    vmem = pl.BlockSpec(memory_space=pltpu.VMEM)
    smem = pl.BlockSpec(memory_space=pltpu.SMEM)
    dma = pltpu.SemaphoreType.DMA

    def matched(mask):
        return pl.pallas_call(
            functools.partial(kernel, mask, tp_bits),
            out_shape=(
                jax.ShapeDtypeStruct((stay + 1, width), bf16),
                jax.ShapeDtypeStruct((1, slots, 1, 2, page, head), bf16),
                jax.ShapeDtypeStruct((stay + 1, width), bf16),
            ),
            in_specs=[pl.BlockSpec(memory_space=pl.ANY)] + [smem] * 4 + [vmem] * 7,
            out_specs=(vmem, vmem, vmem),
            scratch_shapes=[
                pltpu.VMEM((page_count, 2, page, head), bf16),
                pltpu.VMEM((half, 2, page, head), bf16),
                pltpu.VMEM((stay + 1, 8, head), f32),
                pltpu.VMEM((stay + 1, 8, head), f32),
                pltpu.VMEM((8, width), f32),
                pltpu.VMEM((tp_bits, 8, LANES), f32),
                pltpu.VMEM((tp_bits, 8, LANES), f32),
                pltpu.VMEM((16, LANES), bf16),
                pltpu.VMEM((16, LANES), bf16),
                dma((PARTS,)),
                dma((half,)),
                dma((half,)),
                dma((half,)),
                dma((half,)),
                dma((tp_bits,)),
                dma((tp_bits,)),
                dma,
                dma,
            ],
            compiler_params=pltpu.CompilerParams(
                collective_id=mask - 1, has_side_effects=True, vmem_limit_bytes=32 * 1024 * 1024
            ),
            name="matched",
        )

    operands = (
        kv_pool,
        block_table,
        mig_table,
        len_stay,
        len_mig,
        query_stay,
        query_mig,
        new_stay,
        new_mig,
        hidden_stay,
        hidden_mig,
        norm_gain.reshape(1, -1),
    )
    branches = [
        lambda *args, mask=mask: tuple(matched(mask)(*args))
        for mask in range(1, lax.axis_size("inst"))
    ]
    return lax.switch(partner_mask[0] - 1, branches, *operands)


def solution(mesh):
    return jax.shard_map(
        local,
        mesh=mesh,
        in_specs=(
            P("inst", "tp", None, None, None),
            P("inst", None),
            P("inst", None),
            P("inst", "tp"),
            P("inst", "tp"),
            P("inst", "tp", None, None),
            P("inst", "tp", None, None),
            P("inst"),
            P("inst"),
            P("inst", "tp"),
            P("inst", "tp"),
            P("tp"),
            P(),
        ),
        out_specs=(P("inst", "tp"), P("inst", None, "tp", None, None, None), P("inst", "tp")),
        check_vma=False,
    )
```

time: 232 us -> 27.1 us (0.12)
  the two profiles are of different devices: /device:TPU:1 before, /device:TPU:128 now
where the time goes in v1:
time: 27.1 us; the launch traced here: 26.9 us
  Pallas kernels  22.5 us (83%)
  local copies, waits for them, and re-layouts  2.67 us (10%)
  between operations  1.29 us (5%)
  loops' own time  0.47 us (2%)
    pallas_call x1, Pallas kernels, local(): matched(mask)(*args)  22.5 us
    unnamed x3, local copies, waits for them, and re-layouts  1.99 us
    reshape x1, local copies, waits for them, and re-layouts, local(): norm_gain.reshape(1, -1)  0.68 us

profile of v1, /device:TPU:128, one launch (start us, length us, event | category | flops | bytes accessed | tf_op | source)
XLA Modules:
  0.0 26.9 jit_solution(2606293809386457817)
XLA Ops:
  1.3 0.7 %reshape.14 = bf16[1,512]{1,0:T(2,128)(2,1)S(1)} reshape(bf16[512]{0:T(512)(128)(2,1)} %param.55) | data formatting | bytes 2048 | tf_op jit(solution)/shard_map/reshape | solution.py:314
  2.0 23.0 %conditional.1 = ((bf16[7,512]{1,0:T(8,128)(2,1)S(1)}, bf16[1,8,1,2,128,128]{5,4,3,2,1,0:T(8,128)(2,1)S(1)}, bf16[7,512]{1,0:T(8,128)(2,1)S(1)})) conditional(s32[]{:T(128)} %bitcast, (bf16[56,1,2,128,128]{4,3,2,1,0:T(8,128)(2,1)}, s32[6,8]{1,0:T(8,128)}, s32[1,8]{1,0:T(1,128)}, s32[6]{0:T(128)}, s32[1]{0:T(128)}, ...), branch_computations={%region_0.0_spmd, %region_1.0_spmd, %region_2.0_spmd, %region_3.0_... | conditional | bytes 8 | solution.py:320
  2.0 22.5 %matched.33 = (bf16[7,512]{1,0:T(8,128)(2,1)S(1)}, bf16[1,8,1,2,128,128]{5,4,3,2,1,0:T(8,128)(2,1)S(1)}, bf16[7,512]{1,0:T(8,128)(2,1)S(1)}) custom-call(bf16[56,1,2,128,128]{4,3,2,1,0:T(8,128)(2,1)} %get-tuple-element.768.kv_ref, s32[6,8]{1,0:T(8,128)} %get-tuple-element.769.block_table, s32[1,8]{1,0:T(1,128)} %get-tuple-element.770.mig_table, ...), custom_call_target="tpu_custom_call" | custom-call | tf_op jit(solution)/shard_map/cond/branch_2_fun/matched/pallas_call | solution.py:317
  24.9 0.6 %copy.206 = bf16[7,512]{1,0:T(8,128)(2,1)} copy(bf16[7,512]{1,0:T(8,128)(2,1)S(1)} %get-tuple-element.1311) | data formatting | bytes 14336
  25.5 0.8 %copy.207 = bf16[1,8,1,2,128,128]{5,4,3,2,1,0:T(8,128)(2,1)} copy(bf16[1,8,1,2,128,128]{5,4,3,2,1,0:T(8,128)(2,1)S(1)} %get-tuple-element.1312) | data formatting | bytes 1048576
  26.3 0.6 %copy.208 = bf16[7,512]{1,0:T(8,128)(2,1)} copy(bf16[7,512]{1,0:T(8,128)(2,1)S(1)} %get-tuple-element.1313) | data formatting | bytes 14336
